TPU v7x, 512 devices: a whole 4x8x8 slice. The times are simulated.
512 devices in a mesh: tm: 8 (over z), space: 64 (over x, y, core).
Axes of the slice: x: 4, y: 8, z: 8, core: 2. Of those that a mesh axis runs over, the one named last changes fastest.
Arguments:
- right_side: float32 [8, 2048, 2048], P('tm', 'space')
- amp_time: float32 [8], P('tm'), may hold values from 0.5 to 2
- amp_space: float32 [2048], replicated
- lin_sky: float32 [2048, 8, 2048], P('space', 'tm'), may hold values from 0.3 to 3
- tile_row: int32 [8, 4096], P('tm', 'space'), may hold values from 0 to 63, as said below
- tile_col: int32 [8, 4096], P('tm', 'space'), may hold values from 0 to 7
- u_frac: float32 [8, 4096, 128], P('tm', 'space'), may hold values from 0 to 128
- v_frac: float32 [8, 4096, 128], P('tm', 'space'), may hold values from 0 to 16
- noise_weight: float32 [8, 4096, 128], P('tm', 'space'), may hold values from 0.005 to 0.05
Outputs:
- solution: float32 [8, 2048, 2048], P('tm', 'space')
- residual: float32 [8, 2048, 2048], P('tm', 'space')
Inputs may be any that keep to these rules, and one draw needn't show every extreme that they name: `tile_row`: take the blocks in aligned groups of 1 frames by 64 blocks. Within each group, every range of tile rows from r * 1 to r + 1 - 1 is named by exactly 1 block.
All inputs are finite; a program needn't handle non-finite values.
Results may differ from a plain program's by a relative error of at most 0.00055.
Values sent between devices are 32-bit elements; how exact they have to be, the bound alone decides.
A program may use at most 64 MiB of HBM per device.

v0:
```python
import math

import jax
import jax.numpy as jnp
from jax import lax
from jax.sharding import PartitionSpec as P

TV = 16
TU = 128
ITERS = 2


HIGH = lax.Precision.HIGHEST


def band_index(count):
    lower = jnp.arange(count // 4, dtype=jnp.int32)
    return jnp.concatenate([lower, lower + 3 * count // 4])


def angle_tables(row_vals, col_vals, length_all):
    product = row_vals[:, None] * col_vals[None, :] % length_all
    angle = product.astype(jnp.float32) * (2.0 * math.pi / length_all)
    return (jnp.cos(angle), jnp.sin(angle))


def hartley(values, spec_in, spec_out, minor_size, major_size, band_in, band_out):
    length_all = minor_size * major_size
    major_all = jnp.arange(major_size, dtype=jnp.int32)
    minor_all = jnp.arange(minor_size, dtype=jnp.int32)
    columns_in = band_index(major_size) if band_in else major_all
    cos_major, sin_major = angle_tables(major_all, columns_in, major_size)
    middle = spec_in.replace("q", "k")
    pattern = spec_in + ",skq->s" + middle
    first = jnp.einsum(pattern, values, jnp.stack([cos_major, sin_major]), precision=HIGH)
    twist_cos, twist_sin = angle_tables(major_all, minor_all, length_all)
    broadcast_dims = [
        major_size if letter == "k" else minor_size if letter == "p" else 1 for letter in middle
    ]
    twist_cos = twist_cos.reshape(broadcast_dims)
    twist_sin = twist_sin.reshape(broadcast_dims)
    real_part = first[0] * twist_cos - first[1] * twist_sin
    imag_part = -(first[1] * twist_cos + first[0] * twist_sin)
    chosen = band_index(minor_size) if band_out else minor_all
    cos_minor, sin_minor = angle_tables(chosen, minor_all, minor_size)
    closing = "s" + middle + ",sjp->" + spec_out
    closing_tables = jnp.stack([cos_minor + sin_minor, sin_minor - cos_minor])
    result = jnp.einsum(closing, jnp.stack([real_part, imag_part]), closing_tables, precision=HIGH)
    return result * (1.0 / math.sqrt(length_all))


def kernel_tables(u_vals, v_vals):
    cells_v = jnp.arange(TV, dtype=jnp.float32)
    cells_u = jnp.arange(TU, dtype=jnp.float32)
    kern_v = jnp.exp(-0.5 * ((cells_v[None, :, None] - v_vals[:, None, :]) / (TV / 4.0)) ** 2)
    kern_u = jnp.exp(-0.5 * ((cells_u[None, None, :] - u_vals[:, :, None]) / (TU / 8.0)) ** 2)
    return (kern_v, kern_u)


def degrid(tile_data, kern_v, kern_u):
    product = jnp.einsum("nvu,nmu->nvm", tile_data, kern_u, precision=HIGH)
    return jnp.sum(product * kern_v, axis=1)


def spread_back(values, kern_v, kern_u):
    return jnp.einsum("nvm,nmu->nvu", kern_v * values[:, None, :], kern_u, precision=HIGH)


def single_sum(value):
    return lax.psum(value, ("tm", "space"))


def shards(
    right_side, amp_time, amp_space, lin_sky, tile_row, tile_col, u_frac, v_frac, noise_weight
):
    frames, rows_loc, width = right_side.shape
    groups = lax.axis_size("space")
    cols_loc = width // groups
    half_width = width // 2
    band_loc = half_width // groups
    blocks_dev = tile_row.shape[1]
    vis_block = u_frac.shape[2]
    block_count = frames * blocks_dev
    per_owner = block_count // groups
    tile_rows = band_loc // TV
    tile_cols = half_width // TU
    tile_total = tile_rows * frames * tile_cols
    position = lax.axis_index("space")
    amp_rows = lax.dynamic_slice_in_dim(amp_space, position * rows_loc, rows_loc)
    prior_scale = amp_time[:, None, None] * amp_rows[None, :, None] * amp_space[None, None, :]
    rows_flat = tile_row.reshape(block_count)
    cols_flat = tile_col.reshape(block_count)
    frame_ids = jnp.repeat(jnp.arange(frames, dtype=jnp.int32), blocks_dev)
    owner_dev = rows_flat // tile_rows
    sort_order = jnp.argsort(owner_dev, stable=True)
    tile_ids = (rows_flat % tile_rows * frames + frame_ids) * tile_cols + cols_flat
    requests = lax.all_to_all(
        tile_ids[sort_order].reshape(groups, per_owner),
        "space",
        split_axis=0,
        concat_axis=0,
        tiled=True,
    )
    picker = (requests == jnp.arange(tile_total, dtype=jnp.int32)[None, :]).astype(jnp.float32)
    u_sorted = u_frac.reshape(block_count, vis_block)[sort_order]
    v_sorted = v_frac.reshape(block_count, vis_block)[sort_order]
    noise_sorted = noise_weight.reshape(block_count, vis_block)[sort_order]
    kern_v, kern_u = kernel_tables(u_sorted, v_sorted)
    solution = jnp.zeros_like(right_side)
    residual = right_side
    direction = right_side
    norm_now = single_sum(jnp.sum(residual * residual))
    for iteration in range(ITERS):
        forward_partial_value = hartley(
            (prior_scale * direction).reshape(frames, rows_loc, width // 32, 32),
            "frqp",
            "jkfr",
            32,
            width // 32,
            False,
            False,
        )
        forward_partial_value = lax.all_to_all(
            forward_partial_value.reshape(width, frames * rows_loc),
            "space",
            split_axis=0,
            concat_axis=1,
            tiled=True,
        )
        forward_partial_value = forward_partial_value.reshape(cols_loc, groups, frames, rows_loc)
        forward_sky_image = hartley(
            forward_partial_value, "cqfp", "cfjk", rows_loc, groups, False, False
        ).reshape(cols_loc, frames, width)
        forward_sky_image = forward_sky_image * lin_sky
        forward_partial_value = hartley(
            forward_sky_image.reshape(cols_loc, frames, width // 32, 32),
            "cfqp",
            "jkfc",
            32,
            width // 32,
            False,
            True,
        )
        forward_partial_value = lax.all_to_all(
            forward_partial_value.reshape(half_width, frames * cols_loc),
            "space",
            split_axis=0,
            concat_axis=1,
            tiled=True,
        )
        forward_partial_value = forward_partial_value.reshape(band_loc, groups, frames, cols_loc)
        forward_uv_grid = hartley(
            forward_partial_value, "vqfp", "vfjk", cols_loc, groups, False, True
        )
        outgoing = jnp.dot(
            picker,
            forward_uv_grid.reshape(band_loc, frames, half_width)
            .reshape(tile_rows, TV, frames, tile_cols, TU)
            .transpose(0, 2, 3, 1, 4)
            .reshape(tile_total, TV * TU),
            precision=HIGH,
        ).reshape(groups, per_owner, TV * TU)
        incoming = lax.all_to_all(outgoing, "space", split_axis=0, concat_axis=0, tiled=True)
        spread = spread_back(
            noise_sorted * degrid(incoming.reshape(block_count, TV, TU), kern_v, kern_u),
            kern_v,
            kern_u,
        )
        returned = lax.all_to_all(
            spread.reshape(groups, per_owner, TV * TU),
            "space",
            split_axis=0,
            concat_axis=0,
            tiled=True,
        )
        partial_value = hartley(
            jnp.dot(picker.T, returned.reshape(block_count, TV * TU), precision=HIGH)
            .reshape(tile_rows, frames, tile_cols, TV, TU)
            .transpose(0, 3, 1, 2, 4)
            .reshape(band_loc, frames, half_width)
            .reshape(band_loc, frames, cols_loc // 2, groups),
            "vfqp",
            "vjfk",
            groups,
            cols_loc,
            True,
            False,
        )
        partial_value = lax.all_to_all(
            partial_value.reshape(band_loc, groups * frames * cols_loc),
            "space",
            split_axis=1,
            concat_axis=0,
            tiled=True,
        )
        partial_value = partial_value.reshape(half_width // 32, 32, frames, cols_loc)
        sky_image = hartley(partial_value, "qpfc", "cfjk", 32, width // 32, True, False).reshape(
            cols_loc, frames, width
        )
        sky_image = sky_image * lin_sky
        partial_value = hartley(
            sky_image.reshape(cols_loc, frames, rows_loc, groups),
            "cfqp",
            "cjfk",
            groups,
            rows_loc,
            False,
            False,
        )
        partial_value = lax.all_to_all(
            partial_value.reshape(cols_loc, groups * frames * rows_loc),
            "space",
            split_axis=1,
            concat_axis=0,
            tiled=True,
        )
        partial_value = partial_value.reshape(width // 32, 32, frames, rows_loc)
        harmonic = hartley(partial_value, "qpfr", "frjk", 32, width // 32, False, False).reshape(
            frames, rows_loc, width
        )
        applied = direction + prior_scale * harmonic
        step_size = norm_now / single_sum(jnp.sum(direction * applied))
        solution = solution + step_size * direction
        residual = residual - step_size * applied
        if iteration + 1 < ITERS:
            norm_next = single_sum(jnp.sum(residual * residual))
            direction = residual + norm_next / norm_now * direction
            norm_now = norm_next
    return (solution, residual)


def solution(mesh):
    in_specs = (
        P("tm", "space", None),
        P("tm"),
        P(),
        P("space", "tm", None),
        P("tm", "space"),
        P("tm", "space"),
        P("tm", "space", None),
        P("tm", "space", None),
        P("tm", "space", None),
    )
    out_specs = (P("tm", "space", None), P("tm", "space", None))
    return jax.shard_map(shards, mesh=mesh, in_specs=in_specs, out_specs=out_specs, check_vma=False)
```

profile of v0, /device:TPU:1, one launch (start us, length us, event | category | flops | bytes accessed | tf_op | source)
XLA Modules:
  0.0 640.7 jit_solution(1428309937170440164)
XLA Ops:
  2.4 1.0 multiply_multiply_fusion.3
  3.8 1.8 convolution_bitcast_fusion.9
  6.9 1.2 reshape.1735
  8.0 11.6 %all-to-all-start.1 = ((f32[64,1,1024]{2,1,0:T(1,128)}), f32[64,1,1024]{2,1,0:T(1,128)S(1)}, u32[]{:S(2)}, u32[]{:S(2)}) async-start(f32[64,1,1024]{2,1,0:T(1,128)} %reshape.1735), calls=%async_computation.1 | async-start | bytes 524288 | tf_op jit(solution)/shard_map/all_to_all | solution.py:123
  19.7 2.0 sort.17
  23.4 8.2 %all-to-all-done.1 = f32[64,1,1024]{2,1,0:T(1,128)S(1)} async-done(((f32[64,1,1024]{2,1,0:T(1,128)}), f32[64,1,1024]{2,1,0:T(1,128)S(1)}, u32[]{:S(2)}, u32[]{:S(2)}) %all-to-all-start.1) | async-done | bytes 262176 | tf_op jit(solution)/shard_map/all_to_all | solution.py:123
  31.6 6.3 all-to-all-start
  38.6 1.3 reduce.9
  40.8 1.0 convolution_bitcast_fusion.5
  43.0 1.0 multiply_reduce_fusion.6
  44.4 1.8 convolution_bitcast_fusion.8
  48.2 10.3 %all-to-all-start.2 = ((f32[64,1,512]{2,1,0:T(1,128)}), f32[64,1,512]{2,1,0:T(1,128)S(1)}, u32[]{:S(2)}, u32[]{:S(2)}) async-start(f32[64,1,512]{2,1,0:T(1,128)} %reshape.1737), calls=%async_computation.2 | async-start | bytes 262144 | tf_op jit(solution)/shard_map/all_to_all | solution.py:144
  58.5 1.2 reduce
  59.7 9.1 %all-to-all-done.2 = f32[64,1,512]{2,1,0:T(1,128)S(1)} async-done(((f32[64,1,512]{2,1,0:T(1,128)}), f32[64,1,512]{2,1,0:T(1,128)S(1)}, u32[]{:S(2)}, u32[]{:S(2)}) %all-to-all-start.2) | async-done | bytes 131104 | tf_op jit(solution)/shard_map/all_to_all | solution.py:144
  71.9 1.3 copy.134
  73.2 5.3 all-to-all-start.3
  80.4 15.4 %all-to-all-done.3 = f32[64,1,2048]{2,1,0:T(1,128)S(1)} async-done(((f32[64,1,2048]{2,1,0:T(1,128)}), f32[64,1,2048]{2,1,0:T(1,128)S(1)}, u32[]{:S(2)}, u32[]{:S(2)}) %all-to-all-start.3) | async-done | bytes 524320 | tf_op jit(solution)/shard_map/all_to_all | solution.py:163
  95.7 6.7 %fusion.39 = f32[64,128]{1,0:T(8,128)S(1)} fusion(f32[64,16,128]{2,1,0:T(8,128)S(1)} %bitcast.612, f32[64,128]{1,0:T(8,128)S(1)} %gather_fusion.3, f32[64,128]{1,0:T(8,128)S(1)} %gather_fusion.1), kind=kOutput, calls=%fused_computation.68 | convolution fusion | flops 206299136 | bytes 622592 | tf_op jit(solution)/shard_map/nvu,nmu->nvm/dot_general | solution.py:61
  102.5 5.2 fusion.2
  107.6 6.8 %all-to-all-start.4 = ((f32[64,1,2048]{2,1,0:T(1,128)}), f32[64,1,2048]{2,1,0:T(1,128)S(1)}, u32[]{:S(2)}, u32[]{:S(2)}) async-start(f32[64,1,2048]{2,1,0:T(1,128)} %bitcast.64), calls=%async_computation.4 | async-start | bytes 1048576 | tf_op jit(solution)/shard_map/all_to_all | solution.py:169
  114.9 16.7 %all-to-all-done.4 = f32[64,1,2048]{2,1,0:T(1,128)S(1)} async-done(((f32[64,1,2048]{2,1,0:T(1,128)}), f32[64,1,2048]{2,1,0:T(1,128)S(1)}, u32[]{:S(2)}, u32[]{:S(2)}) %all-to-all-start.4) | async-done | bytes 524320 | tf_op jit(solution)/shard_map/all_to_all | solution.py:169
  134.6 6.3 all-to-all-start.5
  141.1 10.1 %all-to-all-done.5 = f32[64,1,512]{2,1,0:T(1,128)S(1)} async-done(((f32[64,1,512]{2,1,0:T(1,128)}), f32[64,1,512]{2,1,0:T(1,128)S(1)}, u32[]{:S(2)}, u32[]{:S(2)}) %all-to-all-start.5) | async-done | bytes 131104 | tf_op jit(solution)/shard_map/all_to_all | solution.py:189
  154.0 1.2 fusion.23
  155.6 1.0 multiply_reduce_fusion.5
  160.3 16.7 %all_to_all.157 = f32[64,1,1024]{2,1,0:T(1,128)S(1)} all-to-all(f32[64,1,1024]{2,1,0:T(1,128)S(1)} %reshape.1741), channel_id=1, replica_groups=mesh['tm'=8,'space'=64] {'space'}, dimensions={0} | all-to-all | bytes 524288 | tf_op jit(solution)/shard_map/all_to_all | solution.py:210
  177.0 1.3 reduce.12
  179.3 1.0 fusion.91
  180.6 1.2 fusion.21
  182.8 102.5 %all-reduce = (f32[]{:T(128)}, f32[]{:T(128)}) all-reduce(f32[]{:T(128)} %get-tuple-element.5, f32[]{:T(128)} %get-tuple-element.4), channel_id=1, replica_groups=mesh['tm'=8,'space'=64] {'tm','space'}, use_global_device_ids=true, to_apply=%region_1.2 | all-reduce | flops 2 | bytes 16 | tf_op jit(solution)/shard_map/psum | solution.py:70
  287.3 94.5 %psum.30 = f32[]{:T(128)} all-reduce(f32[]{:T(128)} %multiply_reduce_fusion.3), channel_id=1, replica_groups=mesh['tm'=8,'space'=64] {'tm','space'}, use_global_device_ids=true, to_apply=%region_7.8 | all-reduce | flops 1 | bytes 8 | tf_op jit(solution)/shard_map/psum | solution.py:70
  383.7 1.8 convolution_bitcast_fusion.7
  387.2 19.4 %all_to_all.158 = f32[64,1,1024]{2,1,0:T(1,128)S(1)} all-to-all(f32[64,1,1024]{2,1,0:T(1,128)S(1)} %reshape.1743), channel_id=1, replica_groups=mesh['tm'=8,'space'=64] {'space'}, dimensions={0} | all-to-all | bytes 524288 | tf_op jit(solution)/shard_map/all_to_all | solution.py:123
  406.6 1.3 reduce.13
  411.0 1.0 multiply_reduce_fusion.2
  412.4 1.8 convolution_bitcast_fusion.6
  415.5 16.2 %all_to_all.159 = f32[64,1,512]{2,1,0:T(1,128)S(1)} all-to-all(f32[64,1,512]{2,1,0:T(1,128)S(1)} %reshape.1745), channel_id=1, replica_groups=mesh['tm'=8,'space'=64] {'space'}, dimensions={0} | all-to-all | bytes 262144 | tf_op jit(solution)/shard_map/all_to_all | solution.py:144
  435.2 22.0 %all_to_all.160 = f32[64,1,2048]{2,1,0:T(1,128)S(1)} all-to-all(f32[64,1,2048]{2,1,0:T(1,128)S(1)} %copy.157), channel_id=1, replica_groups=mesh['tm'=8,'space'=64] {'space'}, dimensions={0} | all-to-all | bytes 1048576 | tf_op jit(solution)/shard_map/all_to_all | solution.py:163
  457.2 6.7 %fusion.38 = f32[64,128]{1,0:T(8,128)S(1)} fusion(f32[64,16,128]{2,1,0:T(8,128)S(1)} %bitcast.614, f32[64,128]{1,0:T(8,128)S(1)} %gather_fusion.3, f32[64,128]{1,0:T(8,128)S(1)} %gather_fusion.1), kind=kOutput, calls=%fused_computation.67 | convolution fusion | flops 206299136 | bytes 622592 | tf_op jit(solution)/shard_map/nvu,nmu->nvm/dot_general | solution.py:61
  464.0 4.4 fusion
  468.3 23.5 %all_to_all.161 = f32[64,1,2048]{2,1,0:T(1,128)S(1)} all-to-all(f32[64,1,2048]{2,1,0:T(1,128)S(1)} %bitcast.613), channel_id=1, replica_groups=mesh['tm'=8,'space'=64] {'space'}, dimensions={0} | all-to-all | bytes 1048576 | tf_op jit(solution)/shard_map/all_to_all | solution.py:169
  494.2 16.5 %all_to_all.162 = f32[64,1,512]{2,1,0:T(1,128)S(1)} all-to-all(f32[64,1,512]{2,1,0:T(1,128)S(1)} %reshape.1747), channel_id=1, replica_groups=mesh['tm'=8,'space'=64] {'space'}, dimensions={0} | all-to-all | bytes 262144 | tf_op jit(solution)/shard_map/all_to_all | solution.py:189
  513.4 1.2 fusion.19
  515.0 1.0 multiply_reduce_fusion.1
  519.7 16.9 %all_to_all.163 = f32[64,1,1024]{2,1,0:T(1,128)S(1)} all-to-all(f32[64,1,1024]{2,1,0:T(1,128)S(1)} %reshape.1749), channel_id=1, replica_groups=mesh['tm'=8,'space'=64] {'space'}, dimensions={0} | all-to-all | bytes 524288 | tf_op jit(solution)/shard_map/all_to_all | solution.py:210
  536.6 1.3 reduce.16
  540.2 1.2 fusion.17
  542.4 95.8 %psum.31 = f32[]{:T(128)} all-reduce(f32[]{:T(128)} %multiply_reduce_fusion), channel_id=1, replica_groups=mesh['tm'=8,'space'=64] {'tm','space'}, use_global_device_ids=true, to_apply=%region_10.11 | all-reduce | flops 1 | bytes 8 | tf_op jit(solution)/shard_map/psum | solution.py:70
  (149 shorter events, 50.9 us)
Async XLA Ops:
  0.6 77.9 %copy-start = (f32[1,64,128]{2,1,0:T(8,128)S(1)}, f32[1,64,128]{2,1,0:T(8,128)}, u32[]{:S(2)}) copy-start(f32[1,64,128]{2,1,0:T(8,128)} %param.15) | copy-start | bytes 98308
  6.8 12.8 %copy-start.8 = (s32[1,64]{1,0:T(1,128)S(1)}, s32[1,64]{1,0:T(1,128)}, u32[]{:S(2)}) copy-start(s32[1,64]{1,0:T(1,128)} %param.13) | copy-start | bytes 772
  6.8 14.9 %copy-start.2 = (s32[1,64]{1,0:T(1,128)S(1)}, s32[1,64]{1,0:T(1,128)}, u32[]{:S(2)}) copy-start(s32[1,64]{1,0:T(1,128)} %param.14) | copy-start | bytes 772
  8.0 23.6 %all-to-all-start.1 = ((f32[64,1,1024]{2,1,0:T(1,128)}), f32[64,1,1024]{2,1,0:T(1,128)S(1)}, u32[]{:S(2)}, u32[]{:S(2)}) async-start(f32[64,1,1024]{2,1,0:T(1,128)} %reshape.1735), calls=%async_computation.1 | async-start | bytes 524288 | tf_op jit(solution)/shard_map/all_to_all | solution.py:123
  31.6 16.5 %all-to-all-start = ((s32[64,1,1]{2,1,0:T(1,128)}), s32[64,1,1]{2,1,0:T(1,128)S(1)}, u32[]{:S(2)}, u32[]{:S(2)}) async-start(s32[64,1,1]{2,1,0:T(1,128)} %copy.122), calls=%async_computation | async-start | bytes 65536 | tf_op jit(solution)/shard_map/all_to_all | solution.py:97
  42.0 1.0 copy-start.4
  48.2 20.7 %all-to-all-start.2 = ((f32[64,1,512]{2,1,0:T(1,128)}), f32[64,1,512]{2,1,0:T(1,128)S(1)}, u32[]{:S(2)}, u32[]{:S(2)}) async-start(f32[64,1,512]{2,1,0:T(1,128)} %reshape.1737), calls=%async_computation.2 | async-start | bytes 262144 | tf_op jit(solution)/shard_map/all_to_all | solution.py:144
  71.9 7.3 %copy-start.5 = (f32[1,64,128]{2,1,0:T(8,128)S(1)}, f32[1,64,128]{2,1,0:T(8,128)}, u32[]{:S(2)}) copy-start(f32[1,64,128]{2,1,0:T(8,128)} %param.16) | copy-start | bytes 98308
  73.2 6.6 %copy-start.6 = (f32[1,64,128]{2,1,0:T(8,128)S(1)}, f32[1,64,128]{2,1,0:T(8,128)}, u32[]{:S(2)}) copy-start(f32[1,64,128]{2,1,0:T(8,128)} %param.17) | copy-start | bytes 98308
  73.2 22.5 %all-to-all-start.3 = ((f32[64,1,2048]{2,1,0:T(1,128)}), f32[64,1,2048]{2,1,0:T(1,128)S(1)}, u32[]{:S(2)}, u32[]{:S(2)}) async-start(f32[64,1,2048]{2,1,0:T(1,128)} %copy.134), calls=%async_computation.3 | async-start | bytes 1048576 | tf_op jit(solution)/shard_map/all_to_all | solution.py:163
  107.6 24.0 %all-to-all-start.4 = ((f32[64,1,2048]{2,1,0:T(1,128)}), f32[64,1,2048]{2,1,0:T(1,128)S(1)}, u32[]{:S(2)}, u32[]{:S(2)}) async-start(f32[64,1,2048]{2,1,0:T(1,128)} %bitcast.64), calls=%async_computation.4 | async-start | bytes 1048576 | tf_op jit(solution)/shard_map/all_to_all | solution.py:169
  134.6 16.6 %all-to-all-start.5 = ((f32[64,1,512]{2,1,0:T(1,128)}), f32[64,1,512]{2,1,0:T(1,128)S(1)}, u32[]{:S(2)}, u32[]{:S(2)}) async-start(f32[64,1,512]{2,1,0:T(1,128)} %reshape.1739), calls=%async_computation.5 | async-start | bytes 262144 | tf_op jit(solution)/shard_map/all_to_all | solution.py:189
  180.6 1.4 copy-start.3
  180.6 1.4 copy-start.7
  541.4 99.0 %copy-start.1 = (f32[1,64,128]{2,1,0:T(8,128)S(1)}, f32[1,64,128]{2,1,0:T(8,128)}, u32[]{:S(2)}) copy-start(f32[1,64,128]{2,1,0:T(8,128)} %param.15) | copy-start | bytes 98308
where the time goes:
time: 647 us; the launch traced here: 641 us
  blocking collectives  424 us (66%)
  waiting for transfers between devices  59.6 us (9%)
  matrix products  54.9 us (8%)
  starting transfers between devices  46.6 us (7%)
  other arithmetic  25.5 us (4%)
  local copies, waits for them, and re-layouts  23.6 us (4%)
  between operations  6.56 us (1%)
    psum x3, blocking collectives, single_sum(): return lax.psum(value, ('tm', 'space'))  293 us
    all_to_all x2, blocking collectives, shards(): lax.all_to_all(partial_value.reshape(cols_loc, groups * frames * rows_loc...  33.6 us
    all_to_all x1, blocking collectives, shards(): lax.all_to_all(spread.reshape(groups, per_owner, TV * TU), 'space', split...  23.5 us
    all_to_all x1, blocking collectives, shards(): lax.all_to_all(outgoing, 'space', split_axis=0, concat_axis=0, tiled=True)  22 us
    all_to_all x1, blocking collectives, shards(): lax.all_to_all(forward_partial_value.reshape(width, frames * rows_loc), '...  19.4 us
    dot_general x16, matrix products, hartley(): jnp.einsum(pattern, values, jnp.stack([cos_major, sin_major]), precision=...  17.6 us
    all_to_all x1, waiting for transfers between devices, shards(): lax.all_to_all(spread.reshape(groups, per_owner, TV * TU), 'space', split...  16.7 us
    all_to_all x1, blocking collectives, shards(): lax.all_to_all(partial_value.reshape(band_loc, groups * frames * cols_loc...  16.5 us
  transfers between devices with their start and end apart: 6, of which 5 were waited for; matrix products, arithmetic and copies ran while one was open for 3% of the time, Pallas kernels for 0%

commit v1 on v0

v1 whole, which is shorter than its diff:
```python
import functools
import math

import jax
import jax.numpy as jnp
import ml_dtypes
import numpy as np
from jax import lax
from jax.experimental import pallas as pl
from jax.experimental.pallas import tpu as pltpu
from jax.sharding import PartitionSpec as P

NX = 2048
GROUPS = 64
ROWS = 32
BAND = 16
BLOCKS = 64
CHUNKS = 32
MESH = pl.DeviceIdType.MESH
F32 = jnp.float32
BF16 = jnp.bfloat16

BAND_TILES = list(range(16)) + list(range(48, 64))
BAND_PARTS = [0, 1, 2, 3, 12, 13, 14, 15]

OFFSETS = [(dx, dy, dc) for dx in range(4) for dy in range(8) for dc in range(2)][1:]
OFFSETS.sort(key=lambda o: -(min(o[0], 4 - o[0]) + min(o[1], 8 - o[1])))


class Graph:
    def __init__(self):
        self.terms = []

    def node(self, *terms):
        self.terms.append(terms)
        return len(self.terms) - 1


def real_fourier(graph, inputs):
    n = len(inputs)
    if n == 1:
        return [(inputs[0], None)]
    if n == 2:
        a, b = inputs
        return [(graph.node((1, a), (1, b)), None), (graph.node((1, a), (-1, b)), None)]
    even = real_fourier(graph, inputs[0::2])
    odd = real_fourier(graph, inputs[1::2])
    out = [None] * (n // 2 + 1)
    e, o = even[0][0], odd[0][0]
    out[0] = (graph.node((1, e), (1, o)), None)
    out[n // 2] = (graph.node((1, e), (-1, o)), None)
    for k in range(1, n // 4):
        cos, sin = math.cos(2 * math.pi * k / n), math.sin(2 * math.pi * k / n)
        er, ei = even[k]
        ore, oim = odd[k]
        tr = graph.node((cos, ore), (sin, oim))
        ti = graph.node((cos, oim), (-sin, ore))
        out[k] = (graph.node((1, er), (1, tr)), graph.node((1, ei), (1, ti)))
        out[n // 2 - k] = (graph.node((1, er), (-1, tr)), graph.node((1, ti), (-1, ei)))
    e, o = even[n // 4][0], odd[n // 4][0]
    out[n // 4] = (e, graph.node((-1, o)))
    return out


def fourier_graph(n):
    graph = Graph()
    inputs = [graph.node() for _ in range(n)]
    return graph, inputs, real_fourier(graph, inputs)


def combine(terms):
    terms = [(c, v) for c, v in terms if v is not None]
    if not terms:
        return None
    terms.sort(key=lambda t: t[0] < 0)
    coef, total = terms[0]
    if coef == -1:
        total = -total
    elif coef != 1:
        total = total * coef
    for coef, value in terms[1:]:
        if coef == 1:
            total = total + value
        elif coef == -1:
            total = total - value
        elif coef < 0:
            total = total - value * (-coef)
        else:
            total = total + value * coef
    return total


def forward_fourier(n, values):
    graph, inputs, outputs = fourier_graph(n)
    known = {}
    for index, terms in enumerate(graph.terms):
        if index < n:
            known[index] = values[index]() if values[index] is not None else None
        else:
            known[index] = combine([(c, known[p]) for c, p in terms])
    return [(known[r], known[i] if i is not None else None) for r, i in outputs]


def transposed_fourier(n, pairs, wanted):
    graph, inputs, outputs = fourier_graph(n)
    needed = set(wanted)
    for index, terms in enumerate(graph.terms):
        if any(p in needed for _, p in terms):
            needed.add(index)
    found = {index: [] for index in range(len(graph.terms))}
    for (r, i), (real, imag) in zip(outputs, pairs):
        found[r].append((1, real))
        if i is not None:
            found[i].append((1, imag))
    result = {}
    for index in reversed(range(len(graph.terms))):
        if index not in needed:
            continue
        value = combine(found[index])
        if index < n:
            result[index] = value
        for coef, parent in graph.terms[index]:
            found[parent].append((coef, value))
    return [result[index] for index in wanted]


def halves(table):
    high = table.astype(ml_dtypes.bfloat16)
    low = (table - high.astype(np.float64)).astype(ml_dtypes.bfloat16)
    return np.stack([high, low])


def long_tables():
    b = np.arange(128)
    theta = 2 * np.pi * (b[None, :] * b[:, None] % 128) / 128
    cos, sin = np.cos(theta), np.sin(theta)
    first = np.concatenate([cos + sin, sin - cos], axis=1)
    second = np.concatenate([cos - sin, cos + sin], axis=1)[::-1]
    main = np.concatenate([first, second], axis=0) / math.sqrt(NX)
    angle = 2 * np.pi * (b[None, :] * (8 + 16 * b[:, None]) % NX) / NX
    edge = np.zeros((256, 256))
    edge[:128, :128] = cos + sin
    edge[128:, 128:] = np.cos(angle) + np.sin(angle)
    edge /= math.sqrt(NX)
    phase = 2 * np.pi * np.arange(8)[:, None] * b[None, :] / NX
    twist = np.stack([np.cos(phase), np.sin(phase)]).astype(np.float32)
    return halves(main), halves(edge), twist


def lane_rows():
    lane = np.arange(128)
    return lane // 32, lane % 32


def lane_band():
    lane = np.arange(128)
    return lane // 16 % 4, lane // 64 * 16 + lane % 16


def short_tables(lanes):
    group_in, index_in = lanes
    group_out, index_out = lane_rows()
    same = group_in[:, None] == group_out[None, :]
    theta = 2 * np.pi * (index_in[:, None] * index_out[None, :] % 32) / 32
    mirrored = 2 * np.pi * (index_in[:, None] * (31 - index_out)[None, :] % 32) / 32
    cos, sin = np.cos(theta), np.sin(theta)
    mcos, msin = np.cos(mirrored), np.sin(mirrored)
    top = np.concatenate([same * (cos + sin), same * (mcos - msin)], axis=1)
    bottom = np.concatenate([same * (sin - cos), same * (mcos + msin)], axis=1)
    main = np.concatenate([top, bottom], axis=0) / math.sqrt(NX)
    phase = 2 * np.pi * np.arange(33)[:, None] * index_in[None, :] / NX
    twist = np.stack([np.cos(phase), np.sin(phase)]).astype(np.float32)
    return halves(main), twist


NN = (((1,), (0,)), ((), ()))
NT = (((1,), (1,)), ((), ()))


def split(x):
    high = x.astype(BF16)
    return high, (x - high.astype(F32)).astype(BF16)


def dot(a, b, dims):
    return lax.dot_general(a, b, dims, preferred_element_type=F32)


def product(x, table, dims):
    high, low = split(x)
    return dot(high, table[0], dims) + (dot(high, table[1], dims) + dot(low, table[0], dims))


def product_left(table, x, dims):
    high, low = split(x)
    return dot(table[0], high, dims) + (dot(table[1], high, dims) + dot(table[0], low, dims))


def long_forward(parts, twist, main, edge):
    spectrum = forward_fourier(16, [None if p is None else (lambda p=p: p) for p in parts])
    rows = [jnp.concatenate([spectrum[0][0], spectrum[8][0]], axis=1)]
    for k in range(1, 8):
        real, imag = spectrum[k]
        cos, sin = twist[0, k : k + 1, :], twist[1, k : k + 1, :]
        rows.append(jnp.concatenate([real * cos + imag * sin, imag * cos - real * sin], axis=1))
    size = rows[0].shape[0]
    data = jnp.concatenate(rows, axis=0)
    out = product_left(main, data, NT)
    special = product_left(edge, data[:128], NT)
    lanes = lax.broadcasted_iota(jnp.int32, (256, 128), 1)
    first = jnp.where(lanes < size, special, out[:, :128])
    if size == 16:
        return first
    return jnp.concatenate([first, out[:, 128:]], axis=1)


def long_backward(data, twist, main, edge, wanted):
    turned = data.T
    size = turned.shape[0] // 8
    out = product(turned, main, NN)
    special = product(turned[:size], edge, NN)
    pairs = [(special[:, :128], None)]
    for k in range(1, 8):
        real, imag = out[k * size : (k + 1) * size, :128], out[k * size : (k + 1) * size, 128:]
        cos, sin = twist[0, k : k + 1, :], twist[1, k : k + 1, :]
        pairs.append((real * cos - imag * sin, real * sin + imag * cos))
    pairs.append((special[:, 128:], None))
    return transposed_fourier(16, pairs, wanted)


def short_in(loaders, twist, store):
    spectrum = forward_fourier(64, loaders)
    for k in range(33):
        real, imag = spectrum[k]
        row = (k - 1) % 32 if k < 32 else 32
        if k == 0:
            store(row, real, jnp.zeros_like(real))
            continue
        cos, sin = twist[0, k : k + 1, :], twist[1, k : k + 1, :]
        if k == 32:
            store(row, real * cos, -(real * sin))
        else:
            store(row, real * cos + imag * sin, imag * cos - real * sin)


def short_out(load, twist, wanted):
    pairs = []
    for k in range(33):
        row = (k - 1) % 32 if k < 32 else 32
        real, imag = load(row)
        if k == 0:
            pairs.append((real, None))
            continue
        cos, sin = twist[0, k : k + 1, :], twist[1, k : k + 1, :]
        if k == 32:
            pairs.append((real * cos - imag * sin, None))
        else:
            pairs.append((real * cos - imag * sin, real * sin + imag * cos))
    return transposed_fourier(64, pairs, wanted)


def fold(tile):
    row = lax.broadcasted_iota(jnp.int32, (8, 128), 0)
    lane = lax.broadcasted_iota(jnp.int32, (8, 128), 1)
    other = pltpu.roll(pltpu.roll(tile, 4, 0), 64, 1)
    return jnp.where((row < 4) == (lane < 64), tile, other)


def kernel(
    right_ref, col_ref, row_ref, lin_ref, trow_ref, tcol_ref, u_ref, v_ref, noise_ref,
    long_ref, edge_ref, ltw_ref, short_ref, shortp_ref, stw_ref, stwp_ref,
    sol_ref, res_ref,
    full_out, full_in, half_out, half_in, vis_out, vis_in, lin_in, red_out, red_in,
    kern_u, kern_v, sky, mid, seen, grid_acc, resid,
    full_s, full_r, half_s, half_r, vis_s, vis_r, lin_s, lin_r, red_s, red_r,
):
    me = lax.axis_index("space")
    frame = lax.axis_index("tm")
    mine = (me // 16, me // 2 % 8, me % 2)

    def at(dx, dy, dc):
        return (mine[0] + dx) % 4 * 16 + (mine[1] + dy) % 8 * 2 + (mine[2] + dc) % 2

    def frame_peer(step):
        return (frame + step) % 8

    barrier = pltpu.get_barrier_semaphore()
    for offset in OFFSETS:
        pl.semaphore_signal(barrier, inc=1, device_id=(frame, at(*offset)), device_id_type=MESH)
    for step in range(1, 8):
        pl.semaphore_signal(barrier, inc=1, device_id=(frame_peer(step), me), device_id_type=MESH)

    def send_all(src, dst, send_sem, recv_sem):
        for offset in OFFSETS:
            other = at(*offset)
            pltpu.make_async_remote_copy(
                src_ref=src.at[other], dst_ref=dst.at[me], send_sem=send_sem, recv_sem=recv_sem,
                device_id=(frame, other), device_id_type=MESH,
            ).start()
        pltpu.make_async_copy(src.at[me], dst.at[me], recv_sem).start()

    def arrived(dst, recv_sem):
        pltpu.make_async_copy(dst, dst, recv_sem).wait()

    def sent(src, count, send_sem):
        part = src.at[pl.ds(0, count)]
        pltpu.make_async_copy(part, part, send_sem).wait()

    def reduce_peer(stage, step):
        if stage == 0:
            return (frame, at(step // 2, 0, step % 2))
        if stage == 1:
            return (frame, at(0, step, 0))
        return (frame_peer(step), me)

    def reduce_send(which, stage, value):
        index = which * 3 + stage
        red_out[index] = value
        for step in range(1, 8):
            pltpu.make_async_remote_copy(
                src_ref=red_out.at[index], dst_ref=red_in.at[index, step - 1],
                send_sem=red_s.at[index], recv_sem=red_r.at[index],
                device_id=reduce_peer(stage, step), device_id_type=MESH,
            ).start()

    def reduce_take(which, stage):
        index = which * 3 + stage
        arrived(red_in.at[index], red_r.at[index])
        return red_out[index] + jnp.sum(red_in[index], axis=0)

    def pack(*values):
        lane = lax.broadcasted_iota(jnp.int32, (8, 128), 1)
        row = lax.broadcasted_iota(jnp.int32, (8, 128), 0)
        total = jnp.zeros((8, 128), F32)
        for index, value in enumerate(values):
            total = total + jnp.where((lane == index) & (row == 0), value, 0.0)
        return total

    def unpack(tile, index):
        return tile[0:1, index : index + 1]

    def whole_sum(x):
        return jnp.sum(jnp.sum(x, axis=0, keepdims=True), axis=1, keepdims=True)

    amp_rows = row_ref[...]

    def scaled(ref, a):
        lanes = slice(128 * a, 128 * (a + 1))
        return ref[:, lanes] * (amp_rows * col_ref[:, lanes])

    def rows_to_columns(ref, n):
        out = long_forward([scaled(ref, a) for a in range(16)], ltw_ref, long_ref, edge_ref)
        for g in range(16):
            for h in range(2):
                for l in range(2):
                    full_out[n, 4 * g + 2 * h + l] = out[
                        128 * h + 8 * g : 128 * h + 8 * g + 8, 128 * l : 128 * (l + 1)
                    ]
        send_all(full_out.at[n], full_in.at[n], full_s.at[n], full_r.at[n])

    def store_mid(row, real, imag):
        mid[8 * row : 8 * row + 8, 0:128] = real
        mid[8 * row : 8 * row + 8, 128:256] = imag

    def load_mid(row):
        return mid[8 * row : 8 * row + 8, 0:128], mid[8 * row : 8 * row + 8, 128:256]

    def through_sky(table_in, table_out):
        image = product(mid[...], table_in, NN) * sky[...]
        mid[...] = product(image, table_out, NT)

    def columns_to_band(n):
        arrived(full_in.at[n], full_r.at[n])
        short_in([lambda s=s: full_in[n, s] for s in range(64)], stw_ref, store_mid)
        through_sky(short_ref, shortp_ref)
        tiles = short_out(load_mid, stwp_ref, BAND_TILES)
        for s, tile in enumerate(tiles):
            folded = fold(tile)
            half_out[n, 2 * s] = folded[0:4]
            half_out[n, 2 * s + 1] = folded[4:8]
        send_all(half_out.at[n], half_in.at[n], half_s.at[n], half_r.at[n])

    def pair_of(n, index):
        return fold(jnp.concatenate([half_in[n, 2 * index], half_in[n, 2 * index + 1]], axis=0))

    def band_to_grid(n):
        arrived(half_in.at[n], half_r.at[n])
        rows = [pair_of(n, 2 * g + h) for h in range(2) for g in range(16)]
        parts = long_backward(
            jnp.concatenate(rows, axis=0), ltw_ref, long_ref, edge_ref, BAND_PARTS
        )
        return jnp.concatenate(parts, axis=0)

    def grid_to_band(grid, n):
        parts = [None] * 16
        for index, a in enumerate(BAND_PARTS):
            parts[a] = grid[BAND * index : BAND * (index + 1)]
        out = long_forward(parts, ltw_ref, long_ref, edge_ref)
        for g in range(16):
            for h in range(2):
                folded = fold(out[128 * h + 8 * g : 128 * h + 8 * g + 8])
                half_out[n, 4 * g + 2 * h] = folded[0:4]
                half_out[n, 4 * g + 2 * h + 1] = folded[4:8]
        send_all(half_out.at[n], half_in.at[n], half_s.at[n], half_r.at[n])

    def band_to_columns(n, m):
        arrived(half_in.at[n], half_r.at[n])
        loaders = [None] * 64
        for index, s in enumerate(BAND_TILES):
            loaders[s] = lambda index=index: pair_of(n, index)
        short_in(loaders, stwp_ref, store_mid)
        through_sky(shortp_ref, short_ref)
        tiles = short_out(load_mid, stw_ref, list(range(64)))
        for s, tile in enumerate(tiles):
            full_out[m, s] = tile
        send_all(full_out.at[m], full_in.at[m], full_s.at[m], full_r.at[m])

    def columns_to_rows(n):
        arrived(full_in.at[n], full_r.at[n])
        data = jnp.concatenate(
            [
                jnp.concatenate(
                    [full_in[n, 4 * g + 2 * h + l] for h in range(2) for g in range(16)], axis=0
                )
                for l in range(2)
            ],
            axis=1,
        )
        parts = long_backward(data, ltw_ref, long_ref, edge_ref, list(range(16)))
        return [
            part * (amp_rows * col_ref[:, 128 * a : 128 * (a + 1)]) for a, part in enumerate(parts)
        ]

    def measure(grid, factor, first):
        high, low = split(grid)
        left = jnp.concatenate(
            [
                jnp.concatenate([high, high], axis=1),
                jnp.concatenate([low, jnp.zeros_like(low)], axis=1),
            ],
            axis=0,
        )
        grid_acc[...] = jnp.zeros((256, 256), F32)

        def step(c, total):
            table = kern_u[c]
            both = dot(left, table, NN)
            weights = kern_v[c]
            values = jnp.sum((both[:128] + both[128:]) * weights, axis=0, keepdims=True)
            if first:
                seen[c] = jnp.broadcast_to(values, (8, 256))
            else:
                values = values + factor * seen[c][0:1]
            noise = jnp.concatenate([vis_in[2 * c, 2:3], vis_in[2 * c + 1, 2:3]], axis=1)
            weighed = noise * values
            up, down = split(weights * weighed)
            grid_acc[...] += dot(jnp.concatenate([up, down], axis=0), table, NT)
            return total + weighed * values

        total = lax.fori_loop(0, CHUNKS, step, jnp.zeros((1, 256), F32))
        acc = grid_acc[...]
        return acc[:128, :128] + (acc[:128, 128:] + acc[128:, :128]), whole_sum(total)

    chosen = lax.broadcasted_iota(jnp.int32, (64, 64), 0) == trow_ref[...]
    picker = chosen.astype(BF16)
    columns = jnp.sum(
        jnp.where(chosen, tcol_ref[...].astype(F32), 0.0), axis=1, keepdims=True
    )
    for index, ref in enumerate((u_ref, v_ref, noise_ref)):
        values = ref[...]
        high = values.astype(BF16)
        rest = values - high.astype(F32)
        middle = rest.astype(BF16)
        low = (rest - middle.astype(F32)).astype(BF16)
        vis_out[:, index, :] = (
            dot(picker, high, NN) + dot(picker, middle, NN)
        ) + dot(picker, low, NN)
    vis_out[:, 3, :] = jnp.broadcast_to(columns, (64, 128))

    right_sum = whole_sum(right_ref[...] * right_ref[...])

    pl.semaphore_wait(barrier, len(OFFSETS) + 7)
    rows_to_columns(right_ref, 0)
    send_all(vis_out, vis_in, vis_s, vis_r)
    place = me % 4
    for step in range(1, 4):
        target = (place + step) % 4
        pltpu.make_async_remote_copy(
            src_ref=lin_ref.at[target], dst_ref=lin_in.at[place], send_sem=lin_s, recv_sem=lin_r,
            device_id=(frame, me - place + target), device_id_type=MESH,
        ).start()
    pltpu.make_async_copy(lin_ref.at[place], lin_in.at[place], lin_r).start()

    arrived(vis_in, vis_r)

    def build(c, carry):
        def pair(index):
            return jnp.concatenate(
                [vis_in[2 * c, index : index + 1], vis_in[2 * c + 1, index : index + 1]], axis=1
            )

        cells = lax.broadcasted_iota(jnp.int32, (128, 256), 0).astype(F32)
        away = (cells - pair(0)) * (8.0 / 128)
        high, low = split(jnp.exp(-0.5 * (away * away)))
        kern_u[c, 0:128] = high
        kern_u[c, 128:256] = low
        cells = lax.broadcasted_iota(jnp.int32, (16, 256), 0).astype(F32)
        away = (cells - pair(1)) * (4.0 / 16)
        values = jnp.exp(-0.5 * (away * away))
        column = pair(3)
        for k in range(8):
            kern_v[c, 16 * k : 16 * k + 16] = jnp.where(column == float(k), values, 0.0)
        return carry

    lax.fori_loop(0, CHUNKS, build, 0)

    arrived(lin_in, lin_r)

    def sky_tile(k):
        return jnp.concatenate([lin_in[r, k] for r in range(4)], axis=0)

    for k in range(1, 32):
        sky[8 * (k - 1) : 8 * k, 0:128] = sky_tile(k)
        sky[8 * (k - 1) : 8 * k, 128:256] = sky_tile(64 - k)
    sky[248:256, 0:128] = sky_tile(0)
    sky[256:264, 0:128] = sky_tile(32)
    sky[248:264, 128:256] = jnp.zeros((16, 128), F32)

    columns_to_band(0)
    grid, weight_sum = measure(band_to_grid(0), None, True)
    reduce_send(0, 0, pack(right_sum, weight_sum))
    grid_to_band(grid, 1)
    reduce_send(0, 1, reduce_take(0, 0))
    band_to_columns(1, 1)
    reduce_send(0, 2, reduce_take(0, 1))
    harmonic = columns_to_rows(1)
    sums = reduce_take(0, 2)
    norm_zero = unpack(sums, 0)
    step_zero = norm_zero / (norm_zero + unpack(sums, 1))
    square = jnp.zeros((32, 128), F32)
    cross = jnp.zeros((32, 128), F32)
    for a in range(16):
        lanes = slice(128 * a, 128 * (a + 1))
        before = right_ref[:, lanes]
        after = before - step_zero * (before + harmonic[a])
        resid[:, lanes] = after
        square = square + after * after
        cross = cross + after * before

    reduce_send(1, 0, pack(whole_sum(square), whole_sum(cross)))
    rows_to_columns(resid, 2)
    reduce_send(1, 1, reduce_take(1, 0))
    columns_to_band(2)
    reduce_send(1, 2, reduce_take(1, 1))
    grid = band_to_grid(2)
    sums = reduce_take(1, 2)
    norm_one = unpack(sums, 0)
    growth = norm_one / norm_zero
    squared = norm_one + 2.0 * growth * unpack(sums, 1) + growth * growth * norm_zero
    grid, weight_sum = measure(grid, growth, False)
    reduce_send(2, 0, pack(weight_sum))
    grid_to_band(grid, 3)
    reduce_send(2, 1, reduce_take(2, 0))
    band_to_columns(3, 3)
    reduce_send(2, 2, reduce_take(2, 1))
    harmonic = columns_to_rows(3)
    sums = reduce_take(2, 2)
    step_one = norm_one / (squared + unpack(sums, 0))
    for a in range(16):
        lanes = slice(128 * a, 128 * (a + 1))
        before = right_ref[:, lanes]
        after = resid[:, lanes]
        direction = after + growth * before
        sol_ref[:, lanes] = step_zero * before + step_one * direction
        res_ref[:, lanes] = after - step_one * (direction + harmonic[a])

    for n in range(4):
        sent(full_out.at[n], 63, full_s.at[n])
        sent(half_out.at[n], 63, half_s.at[n])
    sent(vis_out, 63, vis_s)
    sent(lin_ref, 3, lin_s)
    for index in range(9):
        sent(red_in.at[index], 7, red_s.at[index])


def shards(
    right_side, amp_time, amp_space, lin_sky, tile_row, tile_col, u_frac, v_frac, noise_weight
):
    position = lax.axis_index("space")
    amp_rows = lax.dynamic_slice_in_dim(amp_space, position * ROWS, ROWS) * amp_time[0]
    amp_rows = jnp.broadcast_to(amp_rows[:, None], (ROWS, 128))
    order = np.array(list(range(8)) + [8] + [16 - k for k in range(1, 8)])
    sky = lin_sky.reshape(2, 16, 32, 64)[:, order].reshape(2, 2, 2, 4, 32, 64)
    sky = sky.transpose(1, 2, 5, 0, 3, 4).reshape(4, 64, 2, 128)
    long_main, long_edge, long_twist = long_tables()
    short_main, short_twist = short_tables(lane_rows())
    band_main, band_twist = short_tables(lane_band())
    operands = (
        right_side.reshape(ROWS, NX),
        amp_space.reshape(1, NX),
        amp_rows,
        sky,
        tile_row,
        tile_col,
        u_frac.reshape(BLOCKS, 128),
        v_frac.reshape(BLOCKS, 128),
        noise_weight.reshape(BLOCKS, 128),
        *(
            jnp.asarray(t)
            for t in (
                long_main, long_edge, long_twist, short_main, band_main, short_twist, band_twist,
            )
        ),
    )
    vmem = pl.BlockSpec(memory_space=pltpu.VMEM)
    dma = pltpu.SemaphoreType.DMA
    outs = pl.pallas_call(
        kernel,
        out_shape=[jax.ShapeDtypeStruct((ROWS, NX), F32)] * 2,
        in_specs=[vmem] * len(operands),
        out_specs=[vmem] * 2,
        scratch_shapes=[
            pltpu.VMEM((4, 64, 8, 128), F32),
            pltpu.VMEM((4, 64, 8, 128), F32),
            pltpu.VMEM((4, 64, 4, 128), F32),
            pltpu.VMEM((4, 64, 4, 128), F32),
            pltpu.VMEM((64, 4, 128), F32),
            pltpu.VMEM((64, 4, 128), F32),
            pltpu.VMEM((4, 64, 2, 128), F32),
            pltpu.VMEM((9, 8, 128), F32),
            pltpu.VMEM((9, 7, 8, 128), F32),
            pltpu.VMEM((CHUNKS, 256, 256), BF16),
            pltpu.VMEM((CHUNKS, 128, 256), F32),
            pltpu.VMEM((264, 256), F32),
            pltpu.VMEM((264, 256), F32),
            pltpu.VMEM((CHUNKS, 8, 256), F32),
            pltpu.VMEM((256, 256), F32),
            pltpu.VMEM((ROWS, NX), F32),
            dma((4,)), dma((4,)), dma((4,)), dma((4,)),
            dma, dma, dma, dma,
            dma((9,)), dma((9,)),
        ],
        compiler_params=pltpu.CompilerParams(
            collective_id=0, has_side_effects=True, vmem_limit_bytes=48 * 1024 * 1024
        ),
    )(*operands)
    return tuple(out.reshape(1, ROWS, NX) for out in outs)


def solution(mesh):
    in_specs = (
        P("tm", "space", None),
        P("tm"),
        P(),
        P("space", "tm", None),
        P("tm", "space"),
        P("tm", "space"),
        P("tm", "space", None),
        P("tm", "space", None),
        P("tm", "space", None),
    )
    out_specs = (P("tm", "space", None), P("tm", "space", None))
    return jax.shard_map(shards, mesh=mesh, in_specs=in_specs, out_specs=out_specs, check_vma=False)
```

time: 647 us -> 124 us (0.19)
  blocking collectives: 424 us -> 0 us
  Pallas kernels: 0 us -> 116 us
  waiting for transfers between devices: 59.6 us -> 0 us
  matrix products: 54.9 us -> 0 us
  starting transfers between devices: 46.6 us -> 0 us
  other arithmetic: 25.5 us -> 1.65 us
  local copies, waits for them, and re-layouts: 23.6 us -> 4.24 us
    psum x3 -> x0, blocking collectives: 293 us -> none  [single_sum(): return lax.psum(value, ('tm', 'space'))]
    all_to_all x7 -> x0, blocking collectives: 131 us -> none  [the longest x2 33.6 us: shards(): lax.all_to_all(partial_value.reshape(cols_loc, groups * frames * rows_loc...]
    pallas_call x0 -> x1, Pallas kernels: none -> 116 us  [shards(): pl.pallas_call(kernel, out_shape=[jax.ShapeDtypeStruct((ROWS, NX), F32)]...]
    all_to_all x6 -> x0, waiting for transfers between devices: 59.6 us -> none  [the longest x1 16.7 us: shards(): lax.all_to_all(spread.reshape(groups, per_owner, TV * TU), 'space', split...]
    dot_general x40 -> x0, matrix products: 54.9 us -> none  [the longest x16 17.6 us: hartley(): jnp.einsum(pattern, values, jnp.stack([cos_major, sin_major]), precision=...]
    all_to_all x6 -> x0, starting transfers between devices: 46.6 us -> none  [the longest x1 11.6 us: shards(): lax.all_to_all(forward_partial_value.reshape(width, frames * rows_loc), '...]
    all_to_all x9 -> x0, other arithmetic: 10.4 us -> none  [the longest x2 2.6 us: shards(): lax.all_to_all(partial_value.reshape(cols_loc, groups * frames * rows_loc...]
    all_to_all x14 -> x0, local copies, waits for them, and re-layouts: 7.4 us -> none  [the longest x4 3.05 us: shards(): lax.all_to_all(partial_value.reshape(cols_loc, groups * frames * rows_loc...]
  transfers between devices with their start and end apart: 6 -> 0, of which waited for: 5 -> 0; matrix products, arithmetic and copies ran while one was open for 3% -> 0% of each run, Pallas kernels for 0% -> 0%
where the time goes in v1:
time: 124 us; the launch traced here: 123 us
  Pallas kernels  116 us (94%)
  local copies, waits for them, and re-layouts  4.24 us (3%)
  other arithmetic  1.65 us (1%)
  between operations  1.48 us (1%)
    pallas_call x1, Pallas kernels, shards(): pl.pallas_call(kernel, out_shape=[jax.ShapeDtypeStruct((ROWS, NX), F32)]...  116 us
    unnamed x32, local copies, waits for them, and re-layouts  3.14 us

profile of v1, /device:TPU:1, one launch (start us, length us, event | category | flops | bytes accessed | tf_op | source)
XLA Modules:
  0.0 123.3 jit_solution(13375717358773060425)
XLA Ops:
  0.6 0.0 copy-start.10
  1.3 0.0 copy-done.10
  1.3 0.1 dynamic-slice_multiply_fusion
  1.4 0.0 copy-start.14
  1.4 0.7 copy-done.14
  2.1 0.1 broadcast_in_dim.4.row_ref
  2.1 1.6 %reduce = f32[32,2048]{1,0:T(8,128)S(1)} reduce(f32[32,1,2048]{2,1,0:T(1,128)} %param.21, f32[]{:T(128)} %constant.49), dimensions={1}, to_apply=%param.21.reduce_sub_computation | reduce | bytes 524292 | tf_op args[3]
  3.7 0.2 reshape.37
  3.9 0.6 gather_fusion
  4.5 0.0 copy-start.3
  4.5 0.0 copy-start.4
  4.6 0.0 copy-start.5
  4.6 0.0 copy-start.6
  4.6 0.0 copy-start.7
  4.6 0.0 copy-start.8
  4.6 0.0 copy-start.9
  4.6 0.0 copy-start.11
  4.6 0.0 copy-start.12
  4.6 0.0 copy-start.13
  4.7 0.0 copy-start
  4.7 0.0 copy-start.1
  4.7 0.0 copy-start.2
  4.7 0.2 copy.24.lin_ref
  4.9 0.5 copy-done.3
  5.5 0.1 copy-done.4
  5.6 0.0 copy-done.5
  5.6 0.0 copy-done.6
  5.6 0.0 copy-done.7
  5.6 0.0 copy-done.8
  5.6 0.0 copy-done.9
  5.6 0.0 copy-done.11
  5.6 0.0 copy-done.12
  5.6 0.0 copy-done.13
  5.6 0.2 copy-done
  5.8 0.1 copy-done.1
  5.9 0.1 copy-done.2
  6.0 116.0 %shard_map.185 = (f32[32,2048]{1,0:T(8,128)S(1)}, f32[32,2048]{1,0:T(8,128)S(1)}) custom-call(f32[32,2048]{1,0:T(8,128)S(1)} %bitcast.15, f32[1,2048]{1,0:T(1,128)S(1)} %bitcast.21, f32[32,128]{1,0:T(8,128)S(1)} %broadcast_in_dim.4.row_ref, f32[4,64,2,128]{3,2,1,0:T(2,128)S(1)} %copy.24.lin_ref, s32[1,64]{1,0:T(1,128)S(1)} %copy-done.12, ...), custom_call_target="tpu_custom_call" | custom-call | tf_op jit(solution)/shard_map/pallas_call | solution.py:617
  121.9 0.7 copy.29
  122.6 0.7 copy.30
  (2 shorter events, 0.0 us)
Async XLA Ops:
  0.6 0.7 copy-start.10
  1.4 0.7 copy-start.14
  4.5 1.0 copy-start.3
  4.5 1.0 copy-start.4
  4.6 1.0 copy-start.5
  4.6 1.0 copy-start.6
  4.6 1.0 copy-start.7
  4.6 1.0 copy-start.8
  4.6 1.0 copy-start.9
  4.6 1.0 copy-start.11
  4.6 1.0 copy-start.12
  4.6 1.0 copy-start.13
  4.7 1.1 copy-start
  4.7 1.2 copy-start.1
  4.7 1.2 %copy-start.2 = (bf16[2,256,256]{2,1,0:T(8,128)(2,1)S(1)}, bf16[2,256,256]{2,1,0:T(8,128)(2,1)}, u32[]{:S(2)}) copy-start(bf16[2,256,256]{2,1,0:T(8,128)(2,1)} %constant.35.clone.short_ref) | copy-start | bytes 786436

commit v2 on v1

--- a/solution.py
+++ b/solution.py
@@ -3,7 +3,6 @@
 
 import jax
 import jax.numpy as jnp
-import ml_dtypes
 import numpy as np
 from jax import lax
 from jax.experimental import pallas as pl
@@ -16,6 +15,7 @@
 BAND = 16
 BLOCKS = 64
 CHUNKS = 32
+UNROLL = 16
 MESH = pl.DeviceIdType.MESH
 F32 = jnp.float32
 BF16 = jnp.bfloat16
@@ -124,12 +124,6 @@
     return [result[index] for index in wanted]
 
 
-def halves(table):
-    high = table.astype(ml_dtypes.bfloat16)
-    low = (table - high.astype(np.float64)).astype(ml_dtypes.bfloat16)
-    return np.stack([high, low])
-
-
 def long_tables():
     b = np.arange(128)
     theta = 2 * np.pi * (b[None, :] * b[:, None] % 128) / 128
@@ -144,7 +138,7 @@
     edge /= math.sqrt(NX)
     phase = 2 * np.pi * np.arange(8)[:, None] * b[None, :] / NX
     twist = np.stack([np.cos(phase), np.sin(phase)]).astype(np.float32)
-    return halves(main), halves(edge), twist
+    return main.astype(np.float32), edge.astype(np.float32), twist
 
 
 def lane_rows():
@@ -170,7 +164,7 @@
     main = np.concatenate([top, bottom], axis=0) / math.sqrt(NX)
     phase = 2 * np.pi * np.arange(33)[:, None] * index_in[None, :] / NX
     twist = np.stack([np.cos(phase), np.sin(phase)]).astype(np.float32)
-    return halves(main), twist
+    return main.astype(np.float32), twist
 
 
 NN = (((1,), (0,)), ((), ()))
@@ -267,12 +261,15 @@
 
 
 def kernel(
-    right_ref, col_ref, row_ref, lin_ref, trow_ref, tcol_ref, u_ref, v_ref, noise_ref,
+    right_hbm, time_hbm, col_hbm, lin_hbm, trow_hbm, tcol_hbm, u_hbm, v_hbm, noise_hbm, order_hbm,
+    long_hbm, edge_hbm, ltw_hbm, short_hbm, shortp_hbm, stw_hbm, stwp_hbm,
+    sol_ref, res_ref,
+    right_ref, time_ref, col_ref, raw_ref, trow_ref, tcol_ref, u_ref, v_ref, noise_ref, order_ref,
     long_ref, edge_ref, ltw_ref, short_ref, shortp_ref, stw_ref, stwp_ref,
-    sol_ref, res_ref,
+    long_tab, edge_tab, short_tab, shortp_tab, row_ref, turned, lin_ref,
     full_out, full_in, half_out, half_in, vis_out, vis_in, lin_in, red_out, red_in,
-    kern_u, kern_v, sky, mid, seen, grid_acc, resid,
-    full_s, full_r, half_s, half_r, vis_s, vis_r, lin_s, lin_r, red_s, red_r,
+    kern_u, kern_v, sky, mid, seen, resid,
+    full_s, full_r, half_s, half_r, vis_s, vis_r, lin_s, lin_r, red_s, red_r, load_s,
 ):
     me = lax.axis_index("space")
     frame = lax.axis_index("tm")
@@ -289,6 +286,33 @@
         pl.semaphore_signal(barrier, inc=1, device_id=(frame, at(*offset)), device_id_type=MESH)
     for step in range(1, 8):
         pl.semaphore_signal(barrier, inc=1, device_id=(frame_peer(step), me), device_id_type=MESH)
+
+    loads = [
+        pltpu.make_async_copy(src, dst, load_s.at[index])
+        for index, (src, dst) in enumerate(
+            (
+                (right_hbm.at[0], right_ref),
+                (time_hbm, time_ref),
+                (col_hbm, col_ref),
+                (ltw_hbm, ltw_ref),
+                (long_hbm, long_ref),
+                (edge_hbm, edge_ref),
+                (lin_hbm.at[:, 0, :], raw_ref),
+                (order_hbm, order_ref),
+                (trow_hbm, trow_ref),
+                (tcol_hbm, tcol_ref),
+                (u_hbm.at[0], u_ref),
+                (v_hbm.at[0], v_ref),
+                (noise_hbm.at[0], noise_ref),
+                (short_hbm, short_ref),
+                (shortp_hbm, shortp_ref),
+                (stw_hbm, stw_ref),
+                (stwp_hbm, stwp_ref),
+            )
+        )
+    ]
+    for load in loads:
+        load.start()
 
     def send_all(src, dst, send_sem, recv_sem):
         for offset in OFFSETS:
@@ -342,20 +366,22 @@
     def whole_sum(x):
         return jnp.sum(jnp.sum(x, axis=0, keepdims=True), axis=1, keepdims=True)
 
-    amp_rows = row_ref[...]
+    def scale(a):
+        return row_ref[...] * col_ref[:, 128 * a : 128 * (a + 1)]
 
     def scaled(ref, a):
-        lanes = slice(128 * a, 128 * (a + 1))
-        return ref[:, lanes] * (amp_rows * col_ref[:, lanes])
+        return ref[:, 128 * a : 128 * (a + 1)] * scale(a)
 
     def rows_to_columns(ref, n):
-        out = long_forward([scaled(ref, a) for a in range(16)], ltw_ref, long_ref, edge_ref)
+        out = long_forward([scaled(ref, a) for a in range(16)], ltw_ref, long_tab, edge_tab)
         for g in range(16):
             for h in range(2):
                 for l in range(2):
                     full_out[n, 4 * g + 2 * h + l] = out[
                         128 * h + 8 * g : 128 * h + 8 * g + 8, 128 * l : 128 * (l + 1)
                     ]
+
+    def send_full(n):
         send_all(full_out.at[n], full_in.at[n], full_s.at[n], full_r.at[n])
 
     def store_mid(row, real, imag):
@@ -372,7 +398,7 @@
     def columns_to_band(n):
         arrived(full_in.at[n], full_r.at[n])
         short_in([lambda s=s: full_in[n, s] for s in range(64)], stw_ref, store_mid)
-        through_sky(short_ref, shortp_ref)
+        through_sky(short_tab, shortp_tab)
         tiles = short_out(load_mid, stwp_ref, BAND_TILES)
         for s, tile in enumerate(tiles):
             folded = fold(tile)
@@ -387,7 +413,7 @@
         arrived(half_in.at[n], half_r.at[n])
         rows = [pair_of(n, 2 * g + h) for h in range(2) for g in range(16)]
         parts = long_backward(
-            jnp.concatenate(rows, axis=0), ltw_ref, long_ref, edge_ref, BAND_PARTS
+            jnp.concatenate(rows, axis=0), ltw_ref, long_tab, edge_tab, BAND_PARTS
         )
         return jnp.concatenate(parts, axis=0)
 
@@ -395,7 +421,7 @@
         parts = [None] * 16
         for index, a in enumerate(BAND_PARTS):
             parts[a] = grid[BAND * index : BAND * (index + 1)]
-        out = long_forward(parts, ltw_ref, long_ref, edge_ref)
+        out = long_forward(parts, ltw_ref, long_tab, edge_tab)
         for g in range(16):
             for h in range(2):
                 folded = fold(out[128 * h + 8 * g : 128 * h + 8 * g + 8])
@@ -409,11 +435,11 @@
         for index, s in enumerate(BAND_TILES):
             loaders[s] = lambda index=index: pair_of(n, index)
         short_in(loaders, stwp_ref, store_mid)
-        through_sky(shortp_ref, short_ref)
+        through_sky(shortp_tab, short_tab)
         tiles = short_out(load_mid, stw_ref, list(range(64)))
         for s, tile in enumerate(tiles):
             full_out[m, s] = tile
-        send_all(full_out.at[m], full_in.at[m], full_s.at[m], full_r.at[m])
+        send_full(m)
 
     def columns_to_rows(n):
         arrived(full_in.at[n], full_r.at[n])
@@ -426,62 +452,121 @@
             ],
             axis=1,
         )
-        parts = long_backward(data, ltw_ref, long_ref, edge_ref, list(range(16)))
-        return [
-            part * (amp_rows * col_ref[:, 128 * a : 128 * (a + 1)]) for a, part in enumerate(parts)
-        ]
+        parts = long_backward(data, ltw_ref, long_tab, edge_tab, list(range(16)))
+        return [part * scale(a) for a, part in enumerate(parts)]
 
     def measure(grid, factor, first):
-        high, low = split(grid)
-        left = jnp.concatenate(
-            [
-                jnp.concatenate([high, high], axis=1),
-                jnp.concatenate([low, jnp.zeros_like(low)], axis=1),
-            ],
-            axis=0,
-        )
-        grid_acc[...] = jnp.zeros((256, 256), F32)
-
-        def step(c, total):
-            table = kern_u[c]
-            both = dot(left, table, NN)
-            weights = kern_v[c]
-            values = jnp.sum((both[:128] + both[128:]) * weights, axis=0, keepdims=True)
-            if first:
-                seen[c] = jnp.broadcast_to(values, (8, 256))
-            else:
-                values = values + factor * seen[c][0:1]
-            noise = jnp.concatenate([vis_in[2 * c, 2:3], vis_in[2 * c + 1, 2:3]], axis=1)
-            weighed = noise * values
-            up, down = split(weights * weighed)
-            grid_acc[...] += dot(jnp.concatenate([up, down], axis=0), table, NT)
-            return total + weighed * values
-
-        total = lax.fori_loop(0, CHUNKS, step, jnp.zeros((1, 256), F32))
-        acc = grid_acc[...]
-        return acc[:128, :128] + (acc[:128, 128:] + acc[128:, :128]), whole_sum(total)
-
+        tiles = [grid[BAND * k : BAND * (k + 1)] for k in range(8)]
+        zero = jnp.zeros((BAND, 128), BF16)
+
+        def step(start, carry):
+            total, sums = carry[0], list(carry[1:])
+            for c in [start * UNROLL + index for index in range(UNROLL)]:
+                table = kern_u[c]
+                weights = kern_v[c]
+                columns, rows = [], []
+                for block in (2 * c, 2 * c + 1):
+                    column = vis_in[block, 3:4]
+                    tile = tiles[0]
+                    for k in range(1, 8):
+                        tile = jnp.where(column == float(k), tiles[k], tile)
+                    high, low = split(tile)
+                    columns.append(column)
+                    rows.append(jnp.concatenate([high, high], axis=1))
+                    rows.append(jnp.concatenate([low, zero], axis=1))
+                both = dot(jnp.concatenate(rows, axis=0), table, NN)
+                picked = jnp.concatenate(
+                    [both[0:16, :128] + both[16:32, :128], both[32:48, 128:] + both[48:64, 128:]],
+                    axis=1,
+                )
+                values = jnp.sum(picked * weights, axis=0, keepdims=True)
+                if first:
+                    seen[c] = jnp.broadcast_to(values, (8, 256))
+                else:
+                    values = values + factor * seen[c][0:1]
+                noise = jnp.concatenate([vis_in[2 * c, 2:3], vis_in[2 * c + 1, 2:3]], axis=1)
+                weighed = noise * values
+                total = total + weighed * values
+                up, down = split(weights * weighed)
+                spread = jnp.concatenate(
+                    [
+                        jnp.concatenate([up[:, :128], zero], axis=1),
+                        jnp.concatenate([down[:, :128], zero], axis=1),
+                        jnp.concatenate([zero, up[:, 128:]], axis=1),
+                        jnp.concatenate([zero, down[:, 128:]], axis=1),
+                    ],
+                    axis=0,
+                )
+                back = dot(spread, table, NT)
+                for index, column in enumerate(columns):
+                    high = back[32 * index : 32 * index + 16]
+                    low = back[32 * index + 16 : 32 * index + 32]
+                    tile = high[:, :128] + (high[:, 128:] + low[:, :128])
+                    for k in range(8):
+                        sums[k] = sums[k] + jnp.where(column == float(k), tile, 0.0)
+            return (total, *sums)
+
+        empty = [jnp.zeros((1, 256), F32)] + [jnp.zeros((BAND, 128), F32)] * 8
+        total, *sums = lax.fori_loop(0, CHUNKS // UNROLL, step, tuple(empty))
+        return jnp.concatenate(sums, axis=0), whole_sum(total)
+
+    def exact(picker, values):
+        high = values.astype(BF16)
+        rest = values - high.astype(F32)
+        middle = rest.astype(BF16)
+        low = (rest - middle.astype(F32)).astype(BF16)
+        return (dot(picker, high, NN) + dot(picker, middle, NN)) + dot(picker, low, NN)
+
+    def both_parts(table, parts):
+        parts[0], parts[1] = split(table[...])
+
+    for load in loads[:6]:
+        load.wait()
+    columns = lax.broadcasted_iota(jnp.int32, (ROWS, NX), 1)
+    rows = lax.broadcasted_iota(jnp.int32, (ROWS, NX), 0)
+    amp_rows = jnp.sum(
+        jnp.where(columns == me * ROWS + rows, col_ref[...], 0.0), axis=1, keepdims=True
+    )
+    row_ref[...] = jnp.broadcast_to(amp_rows * time_ref[...], (ROWS, 128))
+    both_parts(long_ref, long_tab)
+    both_parts(edge_ref, edge_tab)
+    rows_to_columns(right_ref, 0)
+    right_sum = whole_sum(right_ref[...] * right_ref[...])
+
+    for load in loads[8:13]:
+        load.wait()
     chosen = lax.broadcasted_iota(jnp.int32, (64, 64), 0) == trow_ref[...]
     picker = chosen.astype(BF16)
     columns = jnp.sum(
         jnp.where(chosen, tcol_ref[...].astype(F32), 0.0), axis=1, keepdims=True
     )
     for index, ref in enumerate((u_ref, v_ref, noise_ref)):
-        values = ref[...]
-        high = values.astype(BF16)
-        rest = values - high.astype(F32)
-        middle = rest.astype(BF16)
-        low = (rest - middle.astype(F32)).astype(BF16)
-        vis_out[:, index, :] = (
-            dot(picker, high, NN) + dot(picker, middle, NN)
-        ) + dot(picker, low, NN)
+        vis_out[:, index, :] = exact(picker, ref[...])
     vis_out[:, 3, :] = jnp.broadcast_to(columns, (64, 128))
 
-    right_sum = whole_sum(right_ref[...] * right_ref[...])
-
+    for load in loads[6:8]:
+        load.wait()
+    ordered = exact(order_ref[...].astype(BF16), raw_ref[...])
+    for c in range(16):
+        turned[128 * c : 128 * (c + 1), 0:32] = ordered[:, 128 * c : 128 * (c + 1)].T
+    for a in range(16):
+        four = jnp.concatenate(
+            [turned[pl.ds(4 * a + r, 32, stride=64), 0:32] for r in range(4)], axis=1
+        )
+        back = four.T
+        for r in range(4):
+            tile = jnp.concatenate(
+                [back[32 * r + 8 * k : 32 * r + 8 * k + 8] for k in range(4)], axis=1
+            )
+            for hl in range(4):
+                lin_ref[hl, 4 * a + r] = tile[2 * hl : 2 * hl + 2]
+
+    for load in loads[13:]:
+        load.wait()
+    both_parts(short_ref, short_tab)
+    both_parts(shortp_ref, shortp_tab)
     pl.semaphore_wait(barrier, len(OFFSETS) + 7)
-    rows_to_columns(right_ref, 0)
-    send_all(vis_out, vis_in, vis_s, vis_r)
+    send_full(0)
     place = me % 4
     for step in range(1, 4):
         target = (place + step) % 4
@@ -490,8 +575,7 @@
             device_id=(frame, me - place + target), device_id_type=MESH,
         ).start()
     pltpu.make_async_copy(lin_ref.at[place], lin_in.at[place], lin_r).start()
-
-    arrived(vis_in, vis_r)
+    send_all(vis_out, vis_in, vis_s, vis_r)
 
     def build(c, carry):
         def pair(index):
@@ -506,13 +590,8 @@
         kern_u[c, 128:256] = low
         cells = lax.broadcasted_iota(jnp.int32, (16, 256), 0).astype(F32)
         away = (cells - pair(1)) * (4.0 / 16)
-        values = jnp.exp(-0.5 * (away * away))
-        column = pair(3)
-        for k in range(8):
-            kern_v[c, 16 * k : 16 * k + 16] = jnp.where(column == float(k), values, 0.0)
+        kern_v[c] = jnp.exp(-0.5 * (away * away))
         return carry
-
-    lax.fori_loop(0, CHUNKS, build, 0)
 
     arrived(lin_in, lin_r)
 
@@ -527,6 +606,8 @@
     sky[248:264, 128:256] = jnp.zeros((16, 128), F32)
 
     columns_to_band(0)
+    arrived(vis_in, vis_r)
+    lax.fori_loop(0, CHUNKS, build, 0)
     grid, weight_sum = measure(band_to_grid(0), None, True)
     reduce_send(0, 0, pack(right_sum, weight_sum))
     grid_to_band(grid, 1)
@@ -549,6 +630,7 @@
 
     reduce_send(1, 0, pack(whole_sum(square), whole_sum(cross)))
     rows_to_columns(resid, 2)
+    send_full(2)
     reduce_send(1, 1, reduce_take(1, 0))
     columns_to_band(2)
     reduce_send(1, 2, reduce_take(1, 1))
@@ -586,25 +668,25 @@
 def shards(
     right_side, amp_time, amp_space, lin_sky, tile_row, tile_col, u_frac, v_frac, noise_weight
 ):
-    position = lax.axis_index("space")
-    amp_rows = lax.dynamic_slice_in_dim(amp_space, position * ROWS, ROWS) * amp_time[0]
-    amp_rows = jnp.broadcast_to(amp_rows[:, None], (ROWS, 128))
-    order = np.array(list(range(8)) + [8] + [16 - k for k in range(1, 8)])
-    sky = lin_sky.reshape(2, 16, 32, 64)[:, order].reshape(2, 2, 2, 4, 32, 64)
-    sky = sky.transpose(1, 2, 5, 0, 3, 4).reshape(4, 64, 2, 128)
+    order = np.zeros((32, 32))
+    for row, (kappa, half, left, k2) in enumerate(np.ndindex(4, 2, 2, 2)):
+        index = 4 * left + kappa
+        k1 = index if half == 0 else 8 if index == 0 else 16 - index
+        order[row, 16 * k2 + k1] = 1.0
     long_main, long_edge, long_twist = long_tables()
     short_main, short_twist = short_tables(lane_rows())
     band_main, band_twist = short_tables(lane_band())
     operands = (
-        right_side.reshape(ROWS, NX),
+        right_side,
+        amp_time.reshape(1, 1),
         amp_space.reshape(1, NX),
-        amp_rows,
-        sky,
+        lin_sky,
         tile_row,
         tile_col,
-        u_frac.reshape(BLOCKS, 128),
-        v_frac.reshape(BLOCKS, 128),
-        noise_weight.reshape(BLOCKS, 128),
+        u_frac,
+        v_frac,
+        noise_weight,
+        jnp.asarray(order, F32),
         *(
             jnp.asarray(t)
             for t in (
@@ -617,9 +699,19 @@
     outs = pl.pallas_call(
         kernel,
         out_shape=[jax.ShapeDtypeStruct((ROWS, NX), F32)] * 2,
-        in_specs=[vmem] * len(operands),
+        in_specs=[pl.BlockSpec(memory_space=pltpu.MemorySpace.HBM)] * len(operands),
         out_specs=[vmem] * 2,
         scratch_shapes=[
+            pltpu.VMEM((ROWS, NX), F32),
+            *(pltpu.VMEM(o.shape, o.dtype) for o in operands[1:3]),
+            pltpu.VMEM((ROWS, NX), F32),
+            *(pltpu.VMEM(o.shape, o.dtype) for o in operands[4:6]),
+            *[pltpu.VMEM((BLOCKS, 128), F32)] * 3,
+            *(pltpu.VMEM(o.shape, o.dtype) for o in operands[9:]),
+            *[pltpu.VMEM((2, 256, 256), BF16)] * 4,
+            pltpu.VMEM((ROWS, 128), F32),
+            pltpu.VMEM((NX, 128), F32),
+            pltpu.VMEM((4, 64, 2, 128), F32),
             pltpu.VMEM((4, 64, 8, 128), F32),
             pltpu.VMEM((4, 64, 8, 128), F32),
             pltpu.VMEM((4, 64, 4, 128), F32),
@@ -630,18 +722,17 @@
             pltpu.VMEM((9, 8, 128), F32),
             pltpu.VMEM((9, 7, 8, 128), F32),
             pltpu.VMEM((CHUNKS, 256, 256), BF16),
-            pltpu.VMEM((CHUNKS, 128, 256), F32),
+            pltpu.VMEM((CHUNKS, BAND, 256), F32),
             pltpu.VMEM((264, 256), F32),
             pltpu.VMEM((264, 256), F32),
             pltpu.VMEM((CHUNKS, 8, 256), F32),
-            pltpu.VMEM((256, 256), F32),
             pltpu.VMEM((ROWS, NX), F32),
             dma((4,)), dma((4,)), dma((4,)), dma((4,)),
             dma, dma, dma, dma,
-            dma((9,)), dma((9,)),
+            dma((9,)), dma((9,)), dma((17,)),
         ],
         compiler_params=pltpu.CompilerParams(
-            collective_id=0, has_side_effects=True, vmem_limit_bytes=48 * 1024 * 1024
+            collective_id=0, has_side_effects=True, vmem_limit_bytes=63 * 1024 * 1024
         ),
     )(*operands)
     return tuple(out.reshape(1, ROWS, NX) for out in outs)

time: 124 us -> 97.4 us (0.79)
  Pallas kernels: 116 us -> 93.6 us
  local copies, waits for them, and re-layouts: 4.24 us -> 2.42 us
  other arithmetic: 1.65 us -> 0 us
    pallas_call x1, Pallas kernels: 116 us -> 93.6 us  [shards(): pl.pallas_call(kernel, out_shape=[jax.ShapeDtypeStruct((ROWS, NX), F32)]...]
    unnamed x1 -> x0, other arithmetic: 1.57 us -> none
    unnamed x32 -> x4, local copies, waits for them, and re-layouts: 3.14 us -> 2.42 us
where the time goes in v2:
time: 97.4 us; the launch traced here: 97.3 us
  Pallas kernels  93.6 us (96%)
  local copies, waits for them, and re-layouts  2.42 us (2%)
  between operations  1.3 us (1%)
    pallas_call x1, Pallas kernels, shards(): pl.pallas_call(kernel, out_shape=[jax.ShapeDtypeStruct((ROWS, NX), F32)]...  93.6 us
    unnamed x4, local copies, waits for them, and re-layouts  2.42 us

profile of v2, /device:TPU:1, one launch (start us, length us, event | category | flops | bytes accessed | tf_op | source)
XLA Modules:
  0.0 97.3 jit_solution(1476512518999364723)
XLA Ops:
  1.3 93.6 %shard_map.176 = (f32[32,2048]{1,0:T(8,128)}, f32[32,2048]{1,0:T(8,128)}) custom-call(f32[1,32,2048]{2,1,0:T(8,128)} %right_hbm.1, f32[1,1]{1,0:T(1,128)} %bitcast.4.time_hbm, f32[1,2048]{1,0:T(1,128)} %bitcast.7, f32[32,1,2048]{2,1,0:T(1,128)} %lin_hbm.1, s32[1,64]{1,0:T(1,128)} %trow_hbm.1, s32[1,64]{1,0:T(1,128)} %tcol_hbm.1, f32[1,64,128]{2,1,0:T(8,128)} %u_hbm.1, ...), custom_call_target="tpu_custom_call" | custom-call | tf_op jit(solution)/shard_map/pallas_call | solution.py:699
  94.9 0.0 copy-start
  94.9 1.7 %copy.22 = f32[1,32,2048]{2,1,0:T(8,128)} copy(f32[1,32,2048]{2,1,0:T(8,128)} %bitcast.6) | data formatting | bytes 524288
  96.6 0.0 copy-done
  96.6 0.7 copy.23
Async XLA Ops:
  94.9 1.7 %copy-start = (f32[32,2048]{1,0:T(8,128)S(1)}, f32[32,2048]{1,0:T(8,128)}, u32[]{:S(2)}) copy-start(f32[32,2048]{1,0:T(8,128)} %get-tuple-element.5) | copy-start | bytes 786436

commit v3 on v2

--- a/solution.py
+++ b/solution.py
@@ -23,8 +23,13 @@
 BAND_TILES = list(range(16)) + list(range(48, 64))
 BAND_PARTS = [0, 1, 2, 3, 12, 13, 14, 15]
 
-OFFSETS = [(dx, dy, dc) for dx in range(4) for dy in range(8) for dc in range(2)][1:]
-OFFSETS.sort(key=lambda o: -(min(o[0], 4 - o[0]) + min(o[1], 8 - o[1])))
+ORDER = [
+    40, 41, 42, 25, 57, 38, 39, 43, 24, 56, 59, 37, 44, 27, 9, 36,
+    23, 22, 8, 45, 26, 54, 58, 55, 10, 7, 21, 34, 47, 46, 29, 35,
+    28, 60, 53, 20, 52, 11, 6, 61, 50, 32, 31, 30, 5, 19, 13, 51,
+    12, 18, 63, 33, 4, 62, 16, 49, 15, 2, 3, 14, 17, 48, 1,
+]
+OFFSETS = [(code // 16, code // 2 % 8, code % 2) for code in ORDER]
 
 
 class Graph:
@@ -268,7 +273,7 @@
     long_ref, edge_ref, ltw_ref, short_ref, shortp_ref, stw_ref, stwp_ref,
     long_tab, edge_tab, short_tab, shortp_tab, row_ref, turned, lin_ref,
     full_out, full_in, half_out, half_in, vis_out, vis_in, lin_in, red_out, red_in,
-    kern_u, kern_v, sky, mid, seen, resid,
+    kern_u, kern_t, kern_v, sky, mid, seen, resid,
     full_s, full_r, half_s, half_r, vis_s, vis_r, lin_s, lin_r, red_s, red_r, load_s,
 ):
     me = lax.axis_index("space")
@@ -497,7 +502,7 @@
                     ],
                     axis=0,
                 )
-                back = dot(spread, table, NT)
+                back = dot(spread, kern_t[c], NN)
                 for index, column in enumerate(columns):
                     high = back[32 * index : 32 * index + 16]
                     low = back[32 * index + 16 : 32 * index + 32]
@@ -585,9 +590,13 @@
 
         cells = lax.broadcasted_iota(jnp.int32, (128, 256), 0).astype(F32)
         away = (cells - pair(0)) * (8.0 / 128)
-        high, low = split(jnp.exp(-0.5 * (away * away)))
+        values = jnp.exp(-0.5 * (away * away))
+        high, low = split(values)
         kern_u[c, 0:128] = high
         kern_u[c, 128:256] = low
+        high, low = split(values.T)
+        kern_t[c, :, 0:128] = high
+        kern_t[c, :, 128:256] = low
         cells = lax.broadcasted_iota(jnp.int32, (16, 256), 0).astype(F32)
         away = (cells - pair(1)) * (4.0 / 16)
         kern_v[c] = jnp.exp(-0.5 * (away * away))
@@ -607,7 +616,7 @@
 
     columns_to_band(0)
     arrived(vis_in, vis_r)
-    lax.fori_loop(0, CHUNKS, build, 0)
+    lax.fori_loop(0, CHUNKS, build, 0, unroll=2)
     grid, weight_sum = measure(band_to_grid(0), None, True)
     reduce_send(0, 0, pack(right_sum, weight_sum))
     grid_to_band(grid, 1)
@@ -722,6 +731,7 @@
             pltpu.VMEM((9, 8, 128), F32),
             pltpu.VMEM((9, 7, 8, 128), F32),
             pltpu.VMEM((CHUNKS, 256, 256), BF16),
+            pltpu.VMEM((CHUNKS, 256, 256), BF16),
             pltpu.VMEM((CHUNKS, BAND, 256), F32),
             pltpu.VMEM((264, 256), F32),
             pltpu.VMEM((264, 256), F32),

time: 97.4 us -> 93.4 us (0.959)
  Pallas kernels: 93.6 us -> 89.6 us
    pallas_call x1, Pallas kernels: 93.6 us -> 89.6 us  [shards(): pl.pallas_call(kernel, out_shape=[jax.ShapeDtypeStruct((ROWS, NX), F32)]...]
where the time goes in v3:
time: 93.4 us; the launch traced here: 93.3 us
  Pallas kernels  89.6 us (96%)
  local copies, waits for them, and re-layouts  2.42 us (3%)
  between operations  1.3 us (1%)
    pallas_call x1, Pallas kernels, shards(): pl.pallas_call(kernel, out_shape=[jax.ShapeDtypeStruct((ROWS, NX), F32)]...  89.6 us
    unnamed x4, local copies, waits for them, and re-layouts  2.42 us

profile of v3, /device:TPU:1, one launch (start us, length us, event | category | flops | bytes accessed | tf_op | source)
XLA Modules:
  0.0 93.3 jit_solution(10067283860378009718)
XLA Ops:
  1.3 89.6 %shard_map.176 = (f32[32,2048]{1,0:T(8,128)}, f32[32,2048]{1,0:T(8,128)}) custom-call(f32[1,32,2048]{2,1,0:T(8,128)} %right_hbm.1, f32[1,1]{1,0:T(1,128)} %bitcast.4.time_hbm, f32[1,2048]{1,0:T(1,128)} %bitcast.7, f32[32,1,2048]{2,1,0:T(1,128)} %lin_hbm.1, s32[1,64]{1,0:T(1,128)} %trow_hbm.1, s32[1,64]{1,0:T(1,128)} %tcol_hbm.1, f32[1,64,128]{2,1,0:T(8,128)} %u_hbm.1, ...), custom_call_target="tpu_custom_call" | custom-call | tf_op jit(solution)/shard_map/pallas_call | solution.py:708
  90.8 0.0 copy-start
  90.9 1.7 %copy.22 = f32[1,32,2048]{2,1,0:T(8,128)} copy(f32[1,32,2048]{2,1,0:T(8,128)} %bitcast.6) | data formatting | bytes 524288
  92.6 0.0 copy-done
  92.6 0.7 copy.23
Async XLA Ops:
  90.8 1.7 %copy-start = (f32[32,2048]{1,0:T(8,128)S(1)}, f32[32,2048]{1,0:T(8,128)}, u32[]{:S(2)}) copy-start(f32[32,2048]{1,0:T(8,128)} %get-tuple-element.5) | copy-start | bytes 786436

commit v4 on v3

--- a/solution.py
+++ b/solution.py
@@ -566,10 +566,6 @@
             for hl in range(4):
                 lin_ref[hl, 4 * a + r] = tile[2 * hl : 2 * hl + 2]
 
-    for load in loads[13:]:
-        load.wait()
-    both_parts(short_ref, short_tab)
-    both_parts(shortp_ref, shortp_tab)
     pl.semaphore_wait(barrier, len(OFFSETS) + 7)
     send_full(0)
     place = me % 4
@@ -581,6 +577,10 @@
         ).start()
     pltpu.make_async_copy(lin_ref.at[place], lin_in.at[place], lin_r).start()
     send_all(vis_out, vis_in, vis_s, vis_r)
+    for load in loads[13:]:
+        load.wait()
+    both_parts(short_ref, short_tab)
+    both_parts(shortp_ref, shortp_tab)
 
     def build(c, carry):
         def pair(index):

time: 93.4 us -> 93.4 us (level)
  no operation moved by 1% of the time
where the time goes in v4:
time: 93.4 us; the launch traced here: 93.3 us
  Pallas kernels  89.6 us (96%)
  local copies, waits for them, and re-layouts  2.42 us (3%)
  between operations  1.3 us (1%)
    pallas_call x1, Pallas kernels, shards(): pl.pallas_call(kernel, out_shape=[jax.ShapeDtypeStruct((ROWS, NX), F32)]...  89.6 us
    unnamed x4, local copies, waits for them, and re-layouts  2.42 us

profile of v4, /device:TPU:1, one launch (start us, length us, event | category | flops | bytes accessed | tf_op | source)
XLA Modules:
  0.0 93.3 jit_solution(10501281029225748632)
XLA Ops:
  1.3 89.6 %shard_map.176 = (f32[32,2048]{1,0:T(8,128)}, f32[32,2048]{1,0:T(8,128)}) custom-call(f32[1,32,2048]{2,1,0:T(8,128)} %right_hbm.1, f32[1,1]{1,0:T(1,128)} %bitcast.4.time_hbm, f32[1,2048]{1,0:T(1,128)} %bitcast.7, f32[32,1,2048]{2,1,0:T(1,128)} %lin_hbm.1, s32[1,64]{1,0:T(1,128)} %trow_hbm.1, s32[1,64]{1,0:T(1,128)} %tcol_hbm.1, f32[1,64,128]{2,1,0:T(8,128)} %u_hbm.1, ...), custom_call_target="tpu_custom_call" | custom-call | tf_op jit(solution)/shard_map/pallas_call | solution.py:708
  90.8 0.0 copy-start
  90.9 1.7 %copy.22 = f32[1,32,2048]{2,1,0:T(8,128)} copy(f32[1,32,2048]{2,1,0:T(8,128)} %bitcast.6) | data formatting | bytes 524288
  92.6 0.0 copy-done
  92.6 0.7 copy.23
Async XLA Ops:
  90.8 1.7 %copy-start = (f32[32,2048]{1,0:T(8,128)S(1)}, f32[32,2048]{1,0:T(8,128)}, u32[]{:S(2)}) copy-start(f32[32,2048]{1,0:T(8,128)} %get-tuple-element.5) | copy-start | bytes 786436
